TPU v7x, 32 devices: a whole 2x2x4 slice. The times are simulated.
32 devices in a mesh: slab: 8 (over y, x, core), view: 4 (over z).
Axes of the slice: x: 2, y: 2, z: 4, core: 2. Of those that a mesh axis runs over, the one named last changes fastest.
Arguments:
- volume: float32 [8, 64, 4096], P('view', 'slab'), may hold values from -6 to 6
- vox_inv: float32 [8, 64, 4096], P('view', 'slab'), may hold values from 0.01 to 0.1
- measured: float32 [128, 12, 4096], P('slab', 'view'), may hold values from -24 to 24
- ray_inv: float32 [128, 12, 4096], P('slab', 'view'), may hold values from 0.05 to 0.5
- col_shift: int32 [12, 8], replicated, may hold values from -512 to 512
- col_frac: float32 [12, 8], replicated, may hold values from 0 to 1
- row_offset: int32 [12, 64], P('view', 'slab'), may hold values from -8 to 8, as said below
- row_frac: float32 [12, 64], P('view', 'slab'), may hold values from 0 to 1
Outputs:
- updated: float32 [8, 64, 4096], P('view', 'slab')
- residual: bfloat16 [128, 12, 4096], P('slab', 'view')
Inputs may be any that keep to these rules, and one draw needn't show every extreme that they name: `row_offset`: every entry lies in -8 to 8, and both ends occur.
All inputs are finite; a program needn't handle non-finite values.
Results may differ from a plain program's by a relative error of at most 0.0095.
Values may be sent and summed in bfloat16 or wider, within the bound.
A program may use at most 64 MiB of HBM per device.

v0:
```python
import jax
import jax.numpy as jnp
from jax import lax
from jax.sharding import PartitionSpec as P


def from_behind(x, axis, by):
    devices = lax.axis_size(axis)
    pairs = [(i, i + by) for i in range(devices) if 0 <= i + by < devices]
    return lax.ppermute(x, axis, pairs)


def with_halo(block, sides, width):
    for axis, dim in sides:
        count = lax.axis_size(axis)
        forward = [(i, i + 1) for i in range(count - 1)]
        backward = [(target, source) for source, target in forward]
        low = lax.ppermute(
            lax.slice_in_dim(block, block.shape[dim] - width, None, axis=dim), axis, forward
        )
        high = lax.ppermute(lax.slice_in_dim(block, 0, width, axis=dim), axis, backward)
        block = jnp.concatenate([low, block, high], axis=dim)
    return block


def band_rows(base, frac, rows):
    r = rows[None, :, None]
    first = jnp.where(r == base[:, None, :], 1.0 - frac[:, None, :], 0.0)
    second = jnp.where(r == base[:, None, :] + 1, frac[:, None, :], 0.0)
    return first + second


def pad_columns(block):
    width = block.shape[-1]
    margin = width // 8 + 1
    widths = [(0, 0)] * (block.ndim - 1) + [(margin, margin)]
    return (jnp.pad(block, widths), margin)


def shear_forward(padded, margin, width, shift, frac):
    count = padded.shape[0]
    total = jnp.zeros((padded.shape[1], width), jnp.float32)
    for line in range(count):
        start = shift[line] + margin
        taps_a = lax.dynamic_slice_in_dim(padded[line], start, width, 1).astype(jnp.float32)
        taps_b = lax.dynamic_slice_in_dim(padded[line], start + 1, width, 1).astype(jnp.float32)
        total = total + (1.0 - frac[line]) * taps_a + frac[line] * taps_b
    return total


def shear_back(padded, margin, width, shift, frac):
    count = shift.shape[0]
    results = []
    for line in range(count):
        start = margin - shift[line]
        taps_a = lax.dynamic_slice_in_dim(padded, start, width, 1).astype(jnp.float32)
        taps_b = lax.dynamic_slice_in_dim(padded, start - 1, width, 1).astype(jnp.float32)
        results.append((1.0 - frac[line]) * taps_a + frac[line] * taps_b)
    return jnp.stack(results)


def per_device(volume, vox_inv, measured, ray_inv, col_shift, col_frac, row_offset, row_frac):
    y_dev, z_dev, width = volume.shape
    row_dev, view_dev = (measured.shape[0], measured.shape[1])
    slab_at = lax.axis_index("slab")
    view_at = lax.axis_index("view")
    own_shift = lax.dynamic_slice_in_dim(col_shift, view_at * view_dev, view_dev, 0)
    own_frac = lax.dynamic_slice_in_dim(col_frac, view_at * view_dev, view_dev, 0)
    z_global = slab_at * z_dev + jnp.arange(z_dev, dtype=jnp.int32)
    base = z_global[None, :] * row_dev // z_dev + row_offset
    lines = volume.astype(jnp.bfloat16)
    piece = lax.all_gather(lines, "view", axis=0, tiled=True)
    padded, add_margin = pad_columns(piece)
    images_now = []
    for view in range(view_dev):
        shift = own_shift[view]
        frac = own_frac[view]
        images_now.append(shear_forward(padded, add_margin, width, shift, frac))
    sheared = jnp.stack(images_now)
    rows = (slab_at - 1) * row_dev + jnp.arange(3 * row_dev, dtype=jnp.int32)
    band = band_rows(base, row_frac, rows)
    local = jnp.einsum("vrz,vzc->rvc", band, sheared, precision=lax.Precision.HIGHEST)
    local = lax.optimization_barrier(local.astype(jnp.bfloat16))
    from_below = from_behind(local[2 * row_dev :], "slab", 1)
    from_above = from_behind(local[:row_dev], "slab", -1)
    projected = (
        local[row_dev : 2 * row_dev].astype(jnp.float32)
        + from_below.astype(jnp.float32)
        + from_above.astype(jnp.float32)
    )
    residual = (ray_inv * (measured - projected)).astype(jnp.bfloat16)
    rim = with_halo(residual, (("slab", 0),), row_dev)
    images = jnp.einsum(
        "vrz,rvc->vzc", band, rim.astype(jnp.float32), precision=lax.Precision.HIGHEST
    )
    images = images.astype(jnp.bfloat16)
    padded_images, margin = pad_columns(images)
    total = jnp.zeros((y_dev * lax.axis_size("view"), z_dev, width), jnp.float32)
    for view in range(view_dev):
        shift = own_shift[view]
        frac = own_frac[view]
        total = total + shear_back(padded_images[view], margin, width, shift, frac)
    back = lax.psum_scatter(
        total.astype(jnp.bfloat16), "view", scatter_dimension=0, tiled=True
    ).astype(jnp.float32)
    updated = volume + vox_inv * back
    return (updated, residual)


def solution(mesh):
    in_specs = (
        P("view", "slab", None),
        P("view", "slab", None),
        P("slab", "view", None),
        P("slab", "view", None),
        P(),
        P(),
        P("view", "slab"),
        P("view", "slab"),
    )
    out_specs = (P("view", "slab", None), P("slab", "view", None))
    return jax.shard_map(
        per_device, mesh=mesh, in_specs=in_specs, out_specs=out_specs, check_vma=False
    )
```

profile of v0, /device:TPU:0, one launch (start us, length us, event | category | flops | bytes accessed | tf_op | source)
XLA Modules:
  0.0 253.2 jit_solution(10525530276075594291)
XLA Ops:
  55.2 0.8 constant_dynamic-slice_fusion.1
  70.8 1.0 convert_element_type.419
  71.8 17.4 %all_gather.3 = bf16[8,8,4096]{2,1,0:T(8,128)(2,1)S(1)} all-gather(bf16[2,8,4096]{2,1,0:T(8,128)(2,1)S(1)} %convert_element_type.419), channel_id=1, replica_groups=mesh['slab'=8,'view'=4] {'view'}, dimensions={0}, use_global_device_ids=true | all-gather | bytes 655360 | tf_op jit(solution)/shard_map/all_gather | solution.py:72
  105.1 5.6 %multiply_add_fusion.1 = f32[1,8,4096]{2,1,0:T(8,128)S(1)} fusion(bf16[1,8,5122]{2,1,0:T(8,128)(2,1)S(1)} %get-tuple-element.13, s32[]{:T(128)S(6)} %select_n.360, f32[]{:T(128)} %bitcast.115, s32[]{:T(128)S(6)} %select_n.359, f32[]{:T(128)S(6)} %sub.400, bf16[1,8,5122]{2,1,0:T(8,128)(2,1)S(1)} %get-tuple-element.12, s32[]{:T(128)S(6)} %select_n.358, ...), kind=kLoop, calls=%fused_computation.51 | loop fusion | flops 1540096 | bytes 1179776 | tf_op jit(solution)/shard_map/add | solution.py:47
  110.7 5.5 %multiply_add_fusion.2 = f32[1,8,4096]{2,1,0:T(8,128)S(1)} fusion(bf16[1,8,5122]{2,1,0:T(8,128)(2,1)S(1)} %get-tuple-element.13, s32[]{:T(128)S(6)} %select_n.344, f32[]{:T(128)} %bitcast.75, s32[]{:T(128)S(6)} %select_n.343, f32[]{:T(128)S(6)} %sub.392, bf16[1,8,5122]{2,1,0:T(8,128)(2,1)S(1)} %get-tuple-element.12, s32[]{:T(128)S(6)} %select_n.342, ...), kind=kLoop, calls=%fused_computation.52 | loop fusion | flops 1540096 | bytes 1179776 | tf_op jit(solution)/shard_map/add | solution.py:47
  116.2 5.6 %multiply_add_fusion.3 = f32[1,8,4096]{2,1,0:T(8,128)S(1)} fusion(bf16[1,8,5122]{2,1,0:T(8,128)(2,1)S(1)} %get-tuple-element.13, s32[]{:T(128)S(6)} %select_n.328, f32[]{:T(128)} %bitcast.35, s32[]{:T(128)S(6)} %select_n.327, f32[]{:T(128)S(6)} %sub.384, bf16[1,8,5122]{2,1,0:T(8,128)(2,1)S(1)} %get-tuple-element.12, s32[]{:T(128)S(6)} %select_n.326, ...), kind=kLoop, calls=%fused_computation.53 | loop fusion | flops 1540096 | bytes 1179776 | tf_op jit(solution)/shard_map/add | solution.py:47
  121.7 2.1 fusion
  123.9 1.4 collective-permute-start.1
  125.4 3.1 %collective-permute-start = (bf16[16,3,4096]{2,0,1:T(8,128)(2,1)S(1)}, bf16[16,3,4096]{2,0,1:T(8,128)(2,1)S(1)}, u32[]{:S(2)}, u32[]{:S(2)}) collective-permute-start(bf16[16,3,4096]{2,0,1:T(8,128)(2,1)S(1)} %get-tuple-element.4), channel_id=1, source_target_pairs={{0,4},{4,8},{8,12},{12,16},{16,20},{20,24},{24,28},{1,5},{5,9},{9,... | collective-permute-start | bytes 1179656 | tf_op jit(solution)/shard_map/ppermute | solution.py:10
  128.4 1.3 collective-permute-done
  129.9 1.3 collective-permute-start.3
  131.2 7.2 %collective-permute-start.2 = (bf16[16,3,4096]{2,0,1:T(8,128)(2,1)S(1)}, bf16[16,3,4096]{2,0,1:T(8,128)(2,1)S(1)}, u32[]{:S(2)}, u32[]{:S(2)}) collective-permute-start(bf16[16,3,4096]{2,0,1:T(8,128)(2,1)S(1)} %multiply_convert_fusion), channel_id=1, source_target_pairs={{0,4},{4,8},{8,12},{12,16},{16,20},{20,24},{24,28},{1,5},{5,9},{9,... | collective-permute-start | bytes 1179656 | tf_op jit(solution)/shard_map/ppermute | solution.py:18
  199.8 0.8 add_dynamic-update-slice_fusion.6
  202.1 0.8 add_dynamic-update-slice_fusion.3
  202.9 0.8 add_dynamic-update-slice_fusion.2
  205.8 0.8 add_dynamic-update-slice_fusion.13
  206.6 0.8 add_dynamic-update-slice_fusion.12
  208.8 0.7 add_dynamic-update-slice_fusion.9
  209.5 0.8 add_dynamic-update-slice_fusion.23
  213.2 0.7 add_dynamic-update-slice_fusion.18
  215.5 1.4 add_dynamic-update-slice_fusion
  216.9 0.9 add_convert_fusion
  217.9 26.8 %reduce-scatter.2.cloned.1.call-done = bf16[2,8,4096]{2,1,0:T(8,128)(2,1)} async-done(((bf16[8,8,4096]{2,1,0:T(8,128)(2,1)}), bf16[2,8,4096]{2,1,0:T(8,128)(2,1)}) %reduce-scatter.2.cloned.1.call-update) | async-done | bytes 131088 | tf_op jit(solution)/shard_map/reduce_scatter | solution.py:103
  244.7 1.6 multiply_add_fusion
  (49 shorter events, 14.6 us)
Async XLA Ops:
  7.2 0.7 copy-start
  7.2 237.5 %reduce-scatter.2.cloned.1.call-start = ((), (), s32[]{:S(2)}) async-start(), calls=%async_computation.1 | async-start | bytes 655360 | tf_op jit(solution)/shard_map/reduce_scatter | solution.py:103
  71.7 32.9 %copy-start.6 = (f32[3,8]{1,0:T(4,128)S(1)}, f32[3,8]{1,0:T(4,128)}, u32[]{:S(2)}) copy-start(f32[3,8]{1,0:T(4,128)} %param.15) | copy-start | bytes 292
  71.7 33.3 %copy-start.7 = (s32[3,8]{1,0:T(4,128)S(1)}, s32[3,8]{1,0:T(4,128)}, u32[]{:S(2)}) copy-start(s32[3,8]{1,0:T(4,128)} %param.14) | copy-start | bytes 292
  123.8 5.9 %copy-start.2 = (f32[16,3,4096]{2,0,1:T(8,128)S(1)}, f32[16,3,4096]{2,0,1:T(8,128)}, u32[]{:S(2)}) copy-start(f32[16,3,4096]{2,0,1:T(8,128)} %param.11) | copy-start | bytes 2359300
  123.9 5.9 %copy-start.3 = (f32[16,3,4096]{2,0,1:T(8,128)S(1)}, f32[16,3,4096]{2,0,1:T(8,128)}, u32[]{:S(2)}) copy-start(f32[16,3,4096]{2,0,1:T(8,128)} %param.10) | copy-start | bytes 2359300
  123.9 4.5 %collective-permute-start.1 = (bf16[16,3,4096]{2,0,1:T(8,128)(2,1)S(1)}, bf16[16,3,4096]{2,0,1:T(8,128)(2,1)S(1)}, u32[]{:S(2)}, u32[]{:S(2)}) collective-permute-start(bf16[16,3,4096]{2,0,1:T(8,128)(2,1)S(1)} %get-tuple-element.5), channel_id=1, source_target_pairs={{4,0},{8,4},{12,8},{16,12},{20,16},{24,20},{28,24},{5,1},{9,5},{13... | collective-permute-start | bytes 1179656 | tf_op jit(solution)/shard_map/ppermute | solution.py:10
  125.4 4.4 %collective-permute-start = (bf16[16,3,4096]{2,0,1:T(8,128)(2,1)S(1)}, bf16[16,3,4096]{2,0,1:T(8,128)(2,1)S(1)}, u32[]{:S(2)}, u32[]{:S(2)}) collective-permute-start(bf16[16,3,4096]{2,0,1:T(8,128)(2,1)S(1)} %get-tuple-element.4), channel_id=1, source_target_pairs={{0,4},{4,8},{8,12},{12,16},{16,20},{20,24},{24,28},{1,5},{5,9},{9,... | collective-permute-start | bytes 1179656 | tf_op jit(solution)/shard_map/ppermute | solution.py:10
  129.9 69.1 %copy-start.4 = (bf16[16,3,4096]{2,0,1:T(8,128)(2,1)}, bf16[16,3,4096]{2,0,1:T(8,128)(2,1)S(1)}, u32[]{:S(2)}) copy-start(bf16[16,3,4096]{2,0,1:T(8,128)(2,1)S(1)} %multiply_convert_fusion) | copy-start | bytes 1179652
  129.9 68.4 %collective-permute-start.3 = (bf16[16,3,4096]{2,0,1:T(8,128)(2,1)S(1)}, bf16[16,3,4096]{2,0,1:T(8,128)(2,1)S(1)}, u32[]{:S(2)}, u32[]{:S(2)}) collective-permute-start(bf16[16,3,4096]{2,0,1:T(8,128)(2,1)S(1)} %multiply_convert_fusion), channel_id=1, source_target_pairs={{4,0},{8,4},{12,8},{16,12},{20,16},{24,20},{28,24},{5,1},{9,5},{13... | collective-permute-start | bytes 1179656 | tf_op jit(solution)/shard_map/ppermute | solution.py:21
  131.2 67.1 %collective-permute-start.2 = (bf16[16,3,4096]{2,0,1:T(8,128)(2,1)S(1)}, bf16[16,3,4096]{2,0,1:T(8,128)(2,1)S(1)}, u32[]{:S(2)}, u32[]{:S(2)}) collective-permute-start(bf16[16,3,4096]{2,0,1:T(8,128)(2,1)S(1)} %multiply_convert_fusion), channel_id=1, source_target_pairs={{0,4},{4,8},{8,12},{12,16},{16,20},{20,24},{24,28},{1,5},{5,9},{9,... | collective-permute-start | bytes 1179656 | tf_op jit(solution)/shard_map/ppermute | solution.py:18
  216.9 27.8 %copy-start.1 = (f32[2,8,4096]{2,1,0:T(8,128)S(1)}, f32[2,8,4096]{2,1,0:T(8,128)}, u32[]{:S(2)}) copy-start(f32[2,8,4096]{2,1,0:T(8,128)} %param.8) | copy-start | bytes 786436
  216.9 27.8 %copy-start.5 = (f32[2,8,4096]{2,1,0:T(8,128)S(1)}, f32[2,8,4096]{2,1,0:T(8,128)}, u32[]{:S(2)}) copy-start(f32[2,8,4096]{2,1,0:T(8,128)} %param.9) | copy-start | bytes 786436
Sparse Core Ops, SparseCore 0:
  218.0 26.6 reduce-scatter.1
where the time goes:
time: 256 us; the launch traced here: 253 us
  between operations  149 us (58%)
  other arithmetic  38 us (15%)
  waiting for transfers between devices  28.2 us (11%)
  blocking collectives  17.4 us (7%)
  starting transfers between devices  13 us (5%)
  local copies, waits for them, and re-layouts  4.51 us (2%)
  matrix products  2.75 us (1%)
    reduce_scatter x1, waiting for transfers between devices, per_device(): lax.psum_scatter(total.astype(jnp.bfloat16), 'view', scatter_dimension=0,...  26.8 us
    all_gather x1, blocking collectives, per_device(): piece = lax.all_gather(lines, 'view', axis=0, tiled=True)  17.4 us
    add x3, other arithmetic, shear_forward(): total = total + (1.0 - frac[line]) * taps_a + frac[line] * taps_b  16.7 us
    unnamed x21, other arithmetic  15.4 us
    ppermute x1, starting transfers between devices, with_halo(): lax.ppermute(lax.slice_in_dim(block, block.shape[dim] - width, None, axis...  7.18 us
  transfers between devices with their start and end apart: 5, of which 2 were waited for; matrix products, arithmetic and copies ran while one was open for 0% of the time, Pallas kernels for 0%

commit v1 on v0

--- a/solution.py
+++ b/solution.py
@@ -69,7 +69,12 @@
     z_global = slab_at * z_dev + jnp.arange(z_dev, dtype=jnp.int32)
     base = z_global[None, :] * row_dev // z_dev + row_offset
     lines = volume.astype(jnp.bfloat16)
-    piece = lax.all_gather(lines, "view", axis=0, tiled=True)
+    ring = [lines]
+    for hop in range(3):
+        ring.append(lax.ppermute(ring[-1], "view", [(dev, (dev + 1) % 4) for dev in range(4)]))
+    piece = jnp.roll(
+        jnp.concatenate(ring[::-1], axis=0), (lax.axis_index("view") + 1) * ring[0].shape[0], axis=0
+    )
     padded, add_margin = pad_columns(piece)
     images_now = []
     for view in range(view_dev):

time: 256 us -> 245 us (0.957)
  blocking collectives: 17.4 us -> 0 us
  starting transfers between devices: 13 us -> 16.8 us
    all_gather x1 -> x0, blocking collectives: 17.4 us -> none  [per_device(): piece = lax.all_gather(lines, 'view', axis=0, tiled=True)]
    ppermute x0 -> x3, starting transfers between devices: none -> 3.82 us  [per_device(): lax.ppermute(ring[-1], 'view', [(dev, (dev + 1) % 4) for dev in range(4)])]
    ppermute x0 -> x3, waiting for transfers between devices: none -> 2.62 us  [per_device(): lax.ppermute(ring[-1], 'view', [(dev, (dev + 1) % 4) for dev in range(4)])]
    unnamed x21 -> x22, other arithmetic: 15.4 us -> 15.4 us
  transfers between devices with their start and end apart: 5 -> 8, of which waited for: 2 -> 4; matrix products, arithmetic and copies ran while one was open for 0% -> 2% of each run, Pallas kernels for 0% -> 0%
where the time goes in v1:
time: 245 us; the launch traced here: 243 us
  between operations  150 us (61%)
  other arithmetic  39.4 us (16%)
  waiting for transfers between devices  29.8 us (12%)
  starting transfers between devices  16.8 us (7%)
  local copies, waits for them, and re-layouts  3.98 us (2%)
  matrix products  2.75 us (1%)
    reduce_scatter x1, waiting for transfers between devices, per_device(): lax.psum_scatter(total.astype(jnp.bfloat16), 'view', scatter_dimension=0,...  25.9 us
    add x3, other arithmetic, shear_forward(): total = total + (1.0 - frac[line]) * taps_a + frac[line] * taps_b  16.6 us
    unnamed x22, other arithmetic  15.4 us
    ppermute x1, starting transfers between devices, with_halo(): lax.ppermute(lax.slice_in_dim(block, block.shape[dim] - width, None, axis...  7.18 us
  transfers between devices with their start and end apart: 8, of which 4 were waited for; matrix products, arithmetic and copies ran while one was open for 2% of the time, Pallas kernels for 0%

profile of v1, /device:TPU:0, one launch (start us, length us, event | category | flops | bytes accessed | tf_op | source)
XLA Modules:
  0.0 242.7 jit_solution(356561872802722578)
XLA Ops:
  7.2 1.0 convert_element_type.419
  8.2 3.1 %collective-permute-start = (bf16[2,8,4096]{2,1,0:T(8,128)(2,1)S(1)}, bf16[2,8,4096]{2,1,0:T(8,128)(2,1)S(1)}, u32[]{:S(2)}, u32[]{:S(2)}) collective-permute-start(bf16[2,8,4096]{2,1,0:T(8,128)(2,1)S(1)} %convert_element_type.419), channel_id=1, source_target_pairs={{0,1},{1,2},{2,3},{3,0},{4,5},{5,6},{6,7},{7,4},{8,9},{9,10},{10,1... | collective-permute-start | bytes 393224 | tf_op jit(solution)/shard_map/ppermute | solution.py:74
  13.4 0.8 constant_dynamic-slice_fusion.2
  14.8 2.0 collective-permute-done
  95.3 5.6 %multiply_add_fusion.1 = f32[1,8,4096]{2,1,0:T(8,128)S(1)} fusion(bf16[1,8,5122]{2,1,0:T(8,128)(2,1)S(1)} %get-tuple-element.13, s32[]{:T(128)S(6)} %select_n.375, f32[]{:T(128)} %bitcast.115, s32[]{:T(128)S(6)} %select_n.374, f32[]{:T(128)S(6)} %sub.405, bf16[1,8,5122]{2,1,0:T(8,128)(2,1)S(1)} %get-tuple-element.12, s32[]{:T(128)S(6)} %select_n.373, ...), kind=kLoop, calls=%fused_computation.51 | loop fusion | flops 1540096 | bytes 1179776 | tf_op jit(solution)/shard_map/add | solution.py:47
  100.8 5.5 %multiply_add_fusion.2 = f32[1,8,4096]{2,1,0:T(8,128)S(1)} fusion(bf16[1,8,5122]{2,1,0:T(8,128)(2,1)S(1)} %get-tuple-element.13, s32[]{:T(128)S(6)} %select_n.359, f32[]{:T(128)} %bitcast.75, s32[]{:T(128)S(6)} %select_n.358, f32[]{:T(128)S(6)} %sub.397, bf16[1,8,5122]{2,1,0:T(8,128)(2,1)S(1)} %get-tuple-element.12, s32[]{:T(128)S(6)} %select_n.357, ...), kind=kLoop, calls=%fused_computation.52 | loop fusion | flops 1540096 | bytes 1179776 | tf_op jit(solution)/shard_map/add | solution.py:47
  106.3 5.6 %multiply_add_fusion.3 = f32[1,8,4096]{2,1,0:T(8,128)S(1)} fusion(bf16[1,8,5122]{2,1,0:T(8,128)(2,1)S(1)} %get-tuple-element.13, s32[]{:T(128)S(6)} %select_n.343, f32[]{:T(128)} %bitcast.35, s32[]{:T(128)S(6)} %select_n.342, f32[]{:T(128)S(6)} %sub.389, bf16[1,8,5122]{2,1,0:T(8,128)(2,1)S(1)} %get-tuple-element.12, s32[]{:T(128)S(6)} %select_n.341, ...), kind=kLoop, calls=%fused_computation.53 | loop fusion | flops 1540096 | bytes 1179776 | tf_op jit(solution)/shard_map/add | solution.py:47
  111.9 2.1 fusion
  114.1 1.4 collective-permute-start.4
  115.5 3.1 %collective-permute-start.3 = (bf16[16,3,4096]{2,0,1:T(8,128)(2,1)S(1)}, bf16[16,3,4096]{2,0,1:T(8,128)(2,1)S(1)}, u32[]{:S(2)}, u32[]{:S(2)}) collective-permute-start(bf16[16,3,4096]{2,0,1:T(8,128)(2,1)S(1)} %get-tuple-element.4), channel_id=1, source_target_pairs={{0,4},{4,8},{8,12},{12,16},{16,20},{20,24},{24,28},{1,5},{5,9},{9,... | collective-permute-start | bytes 1179656 | tf_op jit(solution)/shard_map/ppermute | solution.py:10
  118.6 1.3 collective-permute-done.3
  120.1 1.3 collective-permute-start.6
  121.4 7.2 %collective-permute-start.5 = (bf16[16,3,4096]{2,0,1:T(8,128)(2,1)S(1)}, bf16[16,3,4096]{2,0,1:T(8,128)(2,1)S(1)}, u32[]{:S(2)}, u32[]{:S(2)}) collective-permute-start(bf16[16,3,4096]{2,0,1:T(8,128)(2,1)S(1)} %multiply_convert_fusion), channel_id=1, source_target_pairs={{0,4},{4,8},{8,12},{12,16},{16,20},{20,24},{24,28},{1,5},{5,9},{9,... | collective-permute-start | bytes 1179656 | tf_op jit(solution)/shard_map/ppermute | solution.py:18
  191.1 0.8 add_dynamic-update-slice_fusion.5
  191.9 0.8 add_dynamic-update-slice_fusion.4
  194.1 0.7 add_dynamic-update-slice_fusion.1
  195.5 0.8 add_dynamic-update-slice_fusion.14
  201.3 0.8 add_dynamic-update-slice_fusion.21
  202.8 0.8 add_dynamic-update-slice_fusion.19
  204.4 0.8 add_dynamic-update-slice_fusion.17
  205.9 1.5 add_dynamic-update-slice_fusion
  207.4 0.9 add_convert_fusion
  208.3 25.9 %reduce-scatter.2.cloned.1.call-done = bf16[2,8,4096]{2,1,0:T(8,128)(2,1)} async-done(((bf16[8,8,4096]{2,1,0:T(8,128)(2,1)}), bf16[2,8,4096]{2,1,0:T(8,128)(2,1)}) %reduce-scatter.2.cloned.1.call-update) | async-done | bytes 131088 | tf_op jit(solution)/shard_map/reduce_scatter | solution.py:108
  234.2 1.6 multiply_add_fusion
  (61 shorter events, 17.5 us)
Async XLA Ops:
  7.2 4.2 %copy-start = (s32[12,8]{0,1:T(8,128)S(1)}, s32[12,8]{0,1:T(8,128)}, u32[]{:S(2)}) copy-start(s32[12,8]{0,1:T(8,128)} %param.12) | copy-start | bytes 1156
  7.2 87.7 %copy-start.1 = (f32[2,8,4096]{2,1,0:T(8,128)S(1)}, f32[2,8,4096]{2,1,0:T(8,128)}, u32[]{:S(2)}) copy-start(f32[2,8,4096]{2,1,0:T(8,128)} %param.8) | copy-start | bytes 786436
  7.2 227.0 %reduce-scatter.2.cloned.1.call-start = ((), (), s32[]{:S(2)}) async-start(), calls=%async_computation.1 | async-start | bytes 655360 | tf_op jit(solution)/shard_map/reduce_scatter | solution.py:108
  8.2 8.6 %collective-permute-start = (bf16[2,8,4096]{2,1,0:T(8,128)(2,1)S(1)}, bf16[2,8,4096]{2,1,0:T(8,128)(2,1)S(1)}, u32[]{:S(2)}, u32[]{:S(2)}) collective-permute-start(bf16[2,8,4096]{2,1,0:T(8,128)(2,1)S(1)} %convert_element_type.419), channel_id=1, source_target_pairs={{0,1},{1,2},{2,3},{3,0},{4,5},{5,6},{6,7},{7,4},{8,9},{9,10},{10,1... | collective-permute-start | bytes 393224 | tf_op jit(solution)/shard_map/ppermute | solution.py:74
  16.8 6.8 %collective-permute-start.1 = (bf16[2,8,4096]{2,1,0:T(8,128)(2,1)S(1)}, bf16[2,8,4096]{2,1,0:T(8,128)(2,1)S(1)}, u32[]{:S(2)}, u32[]{:S(2)}) collective-permute-start(bf16[2,8,4096]{2,1,0:T(8,128)(2,1)S(1)} %collective-permute-done), channel_id=1, source_target_pairs={{0,1},{1,2},{2,3},{3,0},{4,5},{5,6},{6,7},{7,4},{8,9},{9,10},{10,1... | collective-permute-start | bytes 393224 | tf_op jit(solution)/shard_map/ppermute | solution.py:74
  23.6 71.2 %collective-permute-start.2 = (bf16[2,8,4096]{2,1,0:T(8,128)(2,1)S(1)}, bf16[2,8,4096]{2,1,0:T(8,128)(2,1)S(1)}, u32[]{:S(2)}, u32[]{:S(2)}) collective-permute-start(bf16[2,8,4096]{2,1,0:T(8,128)(2,1)S(1)} %collective-permute-done.1), channel_id=1, source_target_pairs={{0,1},{1,2},{2,3},{3,0},{4,5},{5,6},{6,7},{7,4},{8,9},{9,10},{10,1... | collective-permute-start | bytes 393224 | tf_op jit(solution)/shard_map/ppermute | solution.py:74
  100.8 11.1 %copy-start.6 = (f32[3,8]{1,0:T(4,128)S(1)}, f32[3,8]{1,0:T(4,128)}, u32[]{:S(2)}) copy-start(f32[3,8]{1,0:T(4,128)} %param.15) | copy-start | bytes 292
  114.0 5.9 %copy-start.2 = (f32[16,3,4096]{2,0,1:T(8,128)S(1)}, f32[16,3,4096]{2,0,1:T(8,128)}, u32[]{:S(2)}) copy-start(f32[16,3,4096]{2,0,1:T(8,128)} %param.11) | copy-start | bytes 2359300
  114.0 5.9 %copy-start.3 = (f32[16,3,4096]{2,0,1:T(8,128)S(1)}, f32[16,3,4096]{2,0,1:T(8,128)}, u32[]{:S(2)}) copy-start(f32[16,3,4096]{2,0,1:T(8,128)} %param.10) | copy-start | bytes 2359300
  114.1 4.5 %collective-permute-start.4 = (bf16[16,3,4096]{2,0,1:T(8,128)(2,1)S(1)}, bf16[16,3,4096]{2,0,1:T(8,128)(2,1)S(1)}, u32[]{:S(2)}, u32[]{:S(2)}) collective-permute-start(bf16[16,3,4096]{2,0,1:T(8,128)(2,1)S(1)} %get-tuple-element.5), channel_id=1, source_target_pairs={{4,0},{8,4},{12,8},{16,12},{20,16},{24,20},{28,24},{5,1},{9,5},{13... | collective-permute-start | bytes 1179656 | tf_op jit(solution)/shard_map/ppermute | solution.py:10
  115.5 4.4 %collective-permute-start.3 = (bf16[16,3,4096]{2,0,1:T(8,128)(2,1)S(1)}, bf16[16,3,4096]{2,0,1:T(8,128)(2,1)S(1)}, u32[]{:S(2)}, u32[]{:S(2)}) collective-permute-start(bf16[16,3,4096]{2,0,1:T(8,128)(2,1)S(1)} %get-tuple-element.4), channel_id=1, source_target_pairs={{0,4},{4,8},{8,12},{12,16},{16,20},{20,24},{24,28},{1,5},{5,9},{9,... | collective-permute-start | bytes 1179656 | tf_op jit(solution)/shard_map/ppermute | solution.py:10
  120.1 69.4 %copy-start.4 = (bf16[16,3,4096]{2,0,1:T(8,128)(2,1)}, bf16[16,3,4096]{2,0,1:T(8,128)(2,1)S(1)}, u32[]{:S(2)}) copy-start(bf16[16,3,4096]{2,0,1:T(8,128)(2,1)S(1)} %multiply_convert_fusion) | copy-start | bytes 1179652
  120.1 68.7 %collective-permute-start.6 = (bf16[16,3,4096]{2,0,1:T(8,128)(2,1)S(1)}, bf16[16,3,4096]{2,0,1:T(8,128)(2,1)S(1)}, u32[]{:S(2)}, u32[]{:S(2)}) collective-permute-start(bf16[16,3,4096]{2,0,1:T(8,128)(2,1)S(1)} %multiply_convert_fusion), channel_id=1, source_target_pairs={{4,0},{8,4},{12,8},{16,12},{20,16},{24,20},{28,24},{5,1},{9,5},{13... | collective-permute-start | bytes 1179656 | tf_op jit(solution)/shard_map/ppermute | solution.py:21
  121.4 67.4 %collective-permute-start.5 = (bf16[16,3,4096]{2,0,1:T(8,128)(2,1)S(1)}, bf16[16,3,4096]{2,0,1:T(8,128)(2,1)S(1)}, u32[]{:S(2)}, u32[]{:S(2)}) collective-permute-start(bf16[16,3,4096]{2,0,1:T(8,128)(2,1)S(1)} %multiply_convert_fusion), channel_id=1, source_target_pairs={{0,4},{4,8},{8,12},{12,16},{16,20},{20,24},{24,28},{1,5},{5,9},{9,... | collective-permute-start | bytes 1179656 | tf_op jit(solution)/shard_map/ppermute | solution.py:18
  207.4 26.9 %copy-start.5 = (f32[2,8,4096]{2,1,0:T(8,128)S(1)}, f32[2,8,4096]{2,1,0:T(8,128)}, u32[]{:S(2)}) copy-start(f32[2,8,4096]{2,1,0:T(8,128)} %param.9) | copy-start | bytes 786436
Sparse Core Ops, SparseCore 0:
  208.5 25.6 reduce-scatter.1
